TPU v7x, 32 devices: a whole 2x2x4 slice. The times are simulated.
32 devices in a mesh: seq: 8 (over z, x), head: 4 (over y, core).
Axes of the slice: x: 2, y: 2, z: 4, core: 2. Of those that a mesh axis runs over, the one named last changes fastest.
Arguments:
- queries: bfloat16 [8192, 4096], P(('seq', 'head')), may hold values from -16 to 16
- keys: bfloat16 [8192, 4096], P(('seq', 'head')), may hold values from -16 to 16
- values: bfloat16 [8192, 4096], P(('seq', 'head')), may hold values from -12 to 12
Outputs:
- attended: bfloat16 [8192, 4096], P(('seq', 'head'))
All inputs are finite; a program needn't handle non-finite values.
Results may differ from a plain program's by a relative error of at most 0.0041.
Values may be sent and summed in bfloat16 or wider, within the bound.
A program may use at most 128 MiB of HBM per device.

v0:
```python
import functools
import math

import jax
import jax.numpy as jnp
from jax import lax
from jax.experimental import pallas as pl
from jax.experimental.pallas import tpu as pltpu
from jax.sharding import PartitionSpec as P

HD = 128
BLOCK = 128


def swapped(x, axis, distance):
    return lax.ppermute(x, axis, [(i, i ^ 1 << distance) for i in range(lax.axis_size(axis))])


def halve(field):
    rows = field.shape[0]
    paired = field.astype(jnp.float32).reshape((rows // 2, 2) + field.shape[1:])
    return ((paired[:, 0] + paired[:, 1]) * 0.5).astype(jnp.bfloat16)


def merge_level(state, level):
    best, numerator, denominator = state
    level_top, level_numerator, level_denominator = level
    joint = jnp.maximum(best, level_top)
    old_weight = jnp.exp(best - joint)
    new_weight = jnp.exp(level_top - joint)
    return (
        joint,
        numerator * old_weight[:, :, None] + level_numerator * new_weight[:, :, None],
        denominator * old_weight + level_denominator * new_weight,
    )


def leaf_level(query, keys_local, values_local, scale):
    length, heads, width = query.shape
    blocks = length // BLOCK
    shaped = (blocks, BLOCK, heads, width)
    scores = (
        jnp.einsum(
            "nigd,njgd->ngij",
            query.reshape(shaped),
            keys_local.reshape(shaped),
            preferred_element_type=jnp.float32,
        )
        * scale
    )
    causal = jnp.arange(BLOCK)[:, None] >= jnp.arange(BLOCK)[None, :]
    top = jnp.max(jnp.where(causal, scores, -jnp.inf), axis=-1)
    weights = jnp.where(causal, jnp.exp(scores - top[..., None]), 0.0)
    numerator = jnp.einsum(
        "ngij,njgd->nigd",
        weights.astype(jnp.bfloat16),
        values_local.reshape(shaped),
        preferred_element_type=jnp.float32,
    )
    denominator = jnp.sum(weights, axis=-1)
    top = top.transpose(0, 2, 1).reshape(length, heads)
    denominator = denominator.transpose(0, 2, 1).reshape(length, heads)
    return (top, numerator.reshape(length, heads, width), denominator)


def pair_level(query, coarse_keys, coarse_values, level, scale):
    length, heads, width = query.shape
    span = BLOCK * 2 ** (level - 1)
    pairs = length // (2 * span)
    upper_queries = query.reshape(pairs, 2, span, heads, width)[:, 1]
    lower_keys = coarse_keys.reshape(pairs, 2, BLOCK, heads, width)[:, 0]
    lower_values = coarse_values.reshape(pairs, 2, BLOCK, heads, width)[:, 0]
    scores = jnp.einsum(
        "npgd,nbgd->npgb", upper_queries, lower_keys, preferred_element_type=jnp.float32
    ) * scale + (level - 1) * math.log(2.0)
    top = jnp.max(scores, axis=-1)
    weights = jnp.exp(scores - top[..., None])
    numerator = jnp.einsum(
        "npgb,nbgd->npgd",
        weights.astype(jnp.bfloat16),
        lower_values,
        preferred_element_type=jnp.float32,
    )
    denominator = jnp.sum(weights, axis=-1)
    top_full = jnp.stack([jnp.full_like(top, -jnp.inf), top], axis=1).reshape(length, heads)
    numerator_full = jnp.stack([jnp.zeros_like(numerator), numerator], axis=1).reshape(
        length, heads, width
    )
    denominator_full = jnp.stack([jnp.zeros_like(denominator), denominator], axis=1).reshape(
        length, heads
    )
    return (top_full, numerator_full, denominator_full)


def far_level(query, tile_keys, tile_values, level, scale, upper):
    length, heads, width = query.shape

    def active():
        scores = jnp.einsum(
            "sgd,bgd->sgb", query, tile_keys, preferred_element_type=jnp.float32
        ) * scale + (level - 1) * math.log(2.0)
        top = jnp.max(scores, axis=-1)
        weights = jnp.exp(scores - top[..., None])
        numerator = jnp.einsum(
            "sgb,bgd->sgd",
            weights.astype(jnp.bfloat16),
            tile_values,
            preferred_element_type=jnp.float32,
        )
        return (top, numerator, jnp.sum(weights, axis=-1))

    def quiet():
        return (
            jnp.full((length, heads), -jnp.inf, jnp.float32),
            jnp.zeros((length, heads, width), jnp.float32),
            jnp.zeros((length, heads), jnp.float32),
        )

    return lax.cond(upper == 1, active, quiet)


def local_part(query, keys_local, values_local, scale):
    state = leaf_level(query, keys_local, values_local, scale)
    depth = (query.shape[0] // BLOCK).bit_length() - 1
    coarse_keys, coarse_values = (keys_local, values_local)
    state = merge_level(state, pair_level(query, coarse_keys, coarse_values, 1, scale))
    coarse_keys = halve(coarse_keys)
    coarse_values = halve(coarse_values)
    return (state, coarse_keys, coarse_values, depth + 1)


def doubling(query, state, tile_keys, tile_values, first, count, position, trade, scale):
    for step in range(count):
        other_keys, other_values = trade(tile_keys, tile_values, step)
        upper = position // 2**step % 2
        state = merge_level(
            state, far_level(query, other_keys, other_values, first + step, scale, upper)
        )
        if step + 1 < count:
            high = upper == 1
            low_keys = jnp.where(high, other_keys, tile_keys)
            high_keys = jnp.where(high, tile_keys, other_keys)
            low_values = jnp.where(high, other_values, tile_values)
            high_values = jnp.where(high, tile_values, other_values)
            tile_keys = halve(jnp.concatenate([low_keys, high_keys], axis=0))
            tile_values = halve(jnp.concatenate([low_values, high_values], axis=0))
    return state


def finish(state):
    best, numerator, denominator = state
    length, heads, width = numerator.shape
    return (numerator / denominator[:, :, None]).astype(jnp.bfloat16).reshape(length, heads * width)


def shards(queries, keys, values):
    scale = 1.0 / math.sqrt(HD)
    length, width = queries.shape
    cube_shape = (length, width // HD, HD)
    query = queries.reshape(cube_shape)
    state, tile_keys, tile_values, first = local_part(
        query, keys.reshape(cube_shape), values.reshape(cube_shape), scale
    )
    position = lax.axis_index(("seq", "head"))
    count = lax.axis_size(("seq", "head")).bit_length() - 1

    def trade_all(send_keys, send_values, bit):
        return swapped((send_keys, send_values), ("seq", "head"), bit)

    state = doubling(query, state, tile_keys, tile_values, first, count, position, trade_all, scale)
    return finish(state)


LEVELS = 5
ORDER = {0: (), 1: (0,), 2: (1, 0), 3: (1, 2, 0), 4: (1, 2, 3, 0)}
COPIES = [(s, i) for s in range(LEVELS) for i in range(-1, s)]
MESH = pl.DeviceIdType.MESH
BASE2 = math.log2(math.e) / math.sqrt(HD)


def halving(rows):
    out = lax.broadcasted_iota(jnp.int32, (rows // 2, rows), 0)
    into = lax.broadcasted_iota(jnp.int32, (rows // 2, rows), 1)
    return jnp.where(into // 2 == out, 0.5, 0.0).astype(jnp.bfloat16)


def scores_of(keys, query):
    return lax.dot_general(keys, query, (((1,), (1,)), ((), ())), preferred_element_type=jnp.float32)


def weighted(values, weights):
    return lax.dot_general(
        values, weights.astype(jnp.bfloat16), (((0,), (0,)), ((), ())), preferred_element_type=jnp.float32
    )


def softened(scores):
    top = jnp.max(scores, axis=0, keepdims=True)
    weights = jnp.exp2((scores - top) * BASE2)
    return top * BASE2, weights, jnp.sum(weights, axis=0, keepdims=True)


def merged(old, new):
    joint = jnp.maximum(old[0], new[0])
    old_weight = jnp.exp2(old[0] - joint)
    new_weight = jnp.exp2(new[0] - joint)
    return (
        joint,
        old[1] * old_weight + new[1] * new_weight,
        old[2] * old_weight + new[2] * new_weight,
    )


def kernel(head_bits, q_ref, k_ref, v_ref, o_ref, *scratch):
    pyramid = scratch[:LEVELS]
    tiles = scratch[LEVELS : 2 * LEVELS]
    numerators, tops, denominators, send_sems, recv_sems = scratch[2 * LEVELS :]
    width = q_ref.shape[1]
    heads = width // HD
    seq, head = lax.axis_index("seq"), lax.axis_index("head")

    def bit(b):
        return head // 2**b % 2 if b < head_bits else seq // 2 ** (b - head_bits) % 2

    def partner(b):
        step = 1 - 2 * bit(b)
        if b < head_bits:
            return (seq, head + step * 2**b)
        return (seq + step * 2 ** (b - head_bits), head)

    def slot(s):
        where = 0
        for i, b in enumerate(ORDER[s]):
            where = where + bit(b) * 2**i
        return where

    def copy(s, i):
        n = COPIES.index((s, i))
        if i < 0:
            source, target, b = pyramid[s], tiles[s].at[slot(s)], s
        else:
            block = pl.ds(slot(s) // 2**i * 2**i, 2**i)
            source = target = tiles[s].at[block]
            b = ORDER[s][i]
        return pltpu.make_async_remote_copy(
            src_ref=source, dst_ref=target, send_sem=send_sems.at[n], recv_sem=recv_sems.at[n],
            device_id=partner(b), device_id_type=MESH,
        )

    def landed(s, i):
        @pl.when(bit(s) == 1)
        def _():
            copy(s, i).wait_recv()
            if i + 1 < s:
                copy(s, i + 1).start()

    barrier = pltpu.get_barrier_semaphore()
    for b in range(LEVELS):
        pl.semaphore_signal(barrier, inc=1, device_id=partner(b), device_id_type=MESH)

    chunk = 512

    @pl.loop(0, width // chunk)
    def _(c):
        columns = pl.ds(pl.multiple_of(c * chunk, chunk), chunk)
        keys, values = k_ref[:, columns], v_ref[:, columns]
        for s in range(LEVELS):
            rows = BLOCK // 2**s
            mean = halving(2 * rows)
            keys = jnp.dot(mean, keys, preferred_element_type=jnp.float32)
            values = jnp.dot(mean, values, preferred_element_type=jnp.float32)
            pyramid[s][:, columns] = jnp.concatenate([keys, values], axis=0).astype(jnp.bfloat16)
            keys, values = keys.astype(jnp.bfloat16), values.astype(jnp.bfloat16)

    pl.semaphore_wait(barrier, LEVELS)
    for s in (1, 2, 3, 4, 0):
        @pl.when(bit(s) == 0)
        def _():
            copy(s, -1).start()

    def columns_of(h):
        return pl.ds(pl.multiple_of(h * HD, HD), HD)

    def store(h, state):
        tops[h] = state[0]
        numerators[h] = state[1]
        denominators[h] = state[2]

    def local(h):
        columns = columns_of(h)
        key = lax.broadcasted_iota(jnp.int32, (BLOCK, BLOCK), 0)
        token = lax.broadcasted_iota(jnp.int32, (BLOCK, BLOCK), 1)
        causal = key <= token
        low, high = pl.ds(0, BLOCK), pl.ds(BLOCK, BLOCK)

        def level(block, rows, mask):
            scores = scores_of(k_ref[rows, columns], q_ref[block, columns])
            if mask:
                scores = jnp.where(causal, scores, -jnp.inf)
            top, weights, total = softened(scores)
            return top, weighted(v_ref[rows, columns], weights), total

        first = level(low, low, True)
        second = merged(level(high, high, True), level(high, low, False))
        store(h, [jnp.concatenate(two, axis=1) for two in zip(first, second)])

    def far(s):
        rows = BLOCK // 2**s

        def of_head(h):
            columns = columns_of(h)
            if rows >= 16:
                keys = tiles[s][:, :rows, columns].reshape(BLOCK, HD)
                values = tiles[s][:, rows:, columns].reshape(BLOCK, HD)
            else:
                both = tiles[s][:, :, columns].astype(jnp.float32)
                keys = both[:, :rows].reshape(BLOCK, HD).astype(jnp.bfloat16)
                values = both[:, rows:].reshape(BLOCK, HD).astype(jnp.bfloat16)
            top, weights, total = softened(scores_of(keys, q_ref[:, columns]))
            level = (top + (s + 1.0), weighted(values, weights), total)
            store(h, merged((tops[h], numerators[h], denominators[h]), level))

        @pl.when(bit(s) == 1)
        def _():
            each(of_head)

    def each(of_head):
        @pl.loop(0, heads // UNROLL)
        def _(g):
            for u in range(UNROLL):
                of_head(g * UNROLL + u)

    def final(h):
        result = numerators[h] / denominators[h]
        o_ref[:, columns_of(h)] = result.T.astype(o_ref.dtype)

    each(local)
    landed(3, -1)
    landed(4, -1)
    landed(0, -1)
    far(0)
    landed(2, -1)
    landed(4, 0)
    landed(3, 0)
    landed(4, 1)
    landed(1, -1)
    landed(3, 1)
    landed(1, 0)
    far(1)
    landed(2, 0)
    landed(4, 2)
    landed(3, 2)
    far(3)
    landed(2, 1)
    far(2)
    landed(4, 3)
    far(4)
    each(final)
    for s, i in COPIES:
        @pl.when(bit(s) == (0 if i < 0 else 1))
        def _():
            copy(s, i).wait_send()


UNROLL = 2


def fused(head_bits, queries, keys, values):
    length, width = queries.shape
    heads = width // HD
    pieces = [(2 * BLOCK // 2**s, width) for s in range(LEVELS)]
    scratch = [pltpu.VMEM(p, jnp.bfloat16) for p in pieces]
    scratch += [pltpu.VMEM((2**s,) + p, jnp.bfloat16) for s, p in enumerate(pieces)]
    scratch += [
        pltpu.VMEM((heads, HD, length), jnp.float32),
        pltpu.VMEM((heads, 1, length), jnp.float32),
        pltpu.VMEM((heads, 1, length), jnp.float32),
        pltpu.SemaphoreType.DMA((len(COPIES),)),
        pltpu.SemaphoreType.DMA((len(COPIES),)),
    ]
    return pl.pallas_call(
        functools.partial(kernel, head_bits),
        out_shape=jax.ShapeDtypeStruct((length, width), jnp.bfloat16),
        in_specs=[pl.BlockSpec(memory_space=pltpu.VMEM)] * 3,
        out_specs=pl.BlockSpec(memory_space=pltpu.VMEM),
        scratch_shapes=scratch,
        compiler_params=pltpu.CompilerParams(
            collective_id=0, has_side_effects=True, vmem_limit_bytes=48 * 2**20
        ),
    )(queries, keys, values)


def solution(mesh):
    if mesh.size == 2**LEVELS:
        body = functools.partial(fused, mesh.shape["head"].bit_length() - 1)
    else:
        body = shards
    return jax.shard_map(
        body,
        mesh=mesh,
        in_specs=(P(("seq", "head"), None), P(("seq", "head"), None), P(("seq", "head"), None)),
        out_specs=P(("seq", "head"), None),
        check_vma=False,
    )
```

profile of v0, /device:TPU:30, one launch (start us, length us, event | category | flops | bytes accessed | tf_op | source)
XLA Modules:
  0.0 101.6 jit_solution(11469235535610359531)
XLA Ops:
  0.0 0.0 copy-start
  0.0 1.6 %copy-done = bf16[256,4096]{1,0:T(8,128)(2,1)S(1)} copy-done((bf16[256,4096]{1,0:T(8,128)(2,1)S(1)}, bf16[256,4096]{1,0:T(8,128)(2,1)}, u32[]{:S(2)}) %copy-start) | copy-done | bytes 2097176
  1.6 98.7 %shard_map.37 = bf16[256,4096]{1,0:T(8,128)(2,1)S(1)} custom-call(bf16[256,4096]{1,0:T(8,128)(2,1)S(1)} %copy-done, bf16[256,4096]{1,0:T(8,128)(2,1)} %k_ref.1, bf16[256,4096]{1,0:T(8,128)(2,1)} %v_ref.1), custom_call_target="tpu_custom_call" | custom-call | tf_op jit(solution)/shard_map/pallas_call | solution.py:381
  100.3 1.3 %copy.5 = bf16[256,4096]{1,0:T(8,128)(2,1)} copy(bf16[256,4096]{1,0:T(8,128)(2,1)S(1)} %shard_map.37) | data formatting | bytes 4194304
Async XLA Ops:
  0.0 1.6 %copy-start = (bf16[256,4096]{1,0:T(8,128)(2,1)S(1)}, bf16[256,4096]{1,0:T(8,128)(2,1)}, u32[]{:S(2)}) copy-start(bf16[256,4096]{1,0:T(8,128)(2,1)} %q_ref.1) | copy-start | bytes 6291460
where the time goes:
time: 102 us
  Pallas kernels  98.7 us (97%)
  local copies, waits for them, and re-layouts  2.91 us (3%)
    pallas_call x1, Pallas kernels, fused(): pl.pallas_call(functools.partial(kernel, head_bits), out_shape=jax.ShapeD...  98.7 us
    unnamed x3, local copies, waits for them, and re-layouts  2.91 us

commit v1 on v0

--- a/solution.py
+++ b/solution.py
@@ -173,7 +173,8 @@
 
 LEVELS = 5
 ORDER = {0: (), 1: (0,), 2: (1, 0), 3: (1, 2, 0), 4: (1, 2, 3, 0)}
-COPIES = [(s, i) for s in range(LEVELS) for i in range(-1, s)]
+PARTS = 2
+COPIES = [(s, i, c) for s in range(LEVELS) for i in range(-1, s) for c in range(PARTS)]
 MESH = pl.DeviceIdType.MESH
 BASE2 = math.log2(math.e) / math.sqrt(HD)
 
@@ -234,25 +235,31 @@
             where = where + bit(b) * 2**i
         return where
 
-    def copy(s, i):
-        n = COPIES.index((s, i))
+    def copy(s, i, c):
+        n = COPIES.index((s, i, c))
+        part = pl.ds(c * (width // PARTS), width // PARTS)
         if i < 0:
-            source, target, b = pyramid[s], tiles[s].at[slot(s)], s
+            source, target, b = pyramid[s].at[:, part], tiles[s].at[slot(s), :, part], s
         else:
             block = pl.ds(slot(s) // 2**i * 2**i, 2**i)
-            source = target = tiles[s].at[block]
+            source = target = tiles[s].at[block, :, part]
             b = ORDER[s][i]
         return pltpu.make_async_remote_copy(
             src_ref=source, dst_ref=target, send_sem=send_sems.at[n], recv_sem=recv_sems.at[n],
             device_id=partner(b), device_id_type=MESH,
         )
 
-    def landed(s, i):
+    def landed(s, i, c):
         @pl.when(bit(s) == 1)
         def _():
-            copy(s, i).wait_recv()
+            copy(s, i, c).wait_recv()
             if i + 1 < s:
-                copy(s, i + 1).start()
+                copy(s, i + 1, c).start()
+
+    def push(s, c):
+        @pl.when(bit(s) == 0)
+        def _():
+            copy(s, -1, c).start()
 
     barrier = pltpu.get_barrier_semaphore()
     for b in range(LEVELS):
@@ -260,109 +267,152 @@
 
     chunk = 512
 
-    @pl.loop(0, width // chunk)
-    def _(c):
-        columns = pl.ds(pl.multiple_of(c * chunk, chunk), chunk)
-        keys, values = k_ref[:, columns], v_ref[:, columns]
-        for s in range(LEVELS):
-            rows = BLOCK // 2**s
-            mean = halving(2 * rows)
-            keys = jnp.dot(mean, keys, preferred_element_type=jnp.float32)
-            values = jnp.dot(mean, values, preferred_element_type=jnp.float32)
-            pyramid[s][:, columns] = jnp.concatenate([keys, values], axis=0).astype(jnp.bfloat16)
-            keys, values = keys.astype(jnp.bfloat16), values.astype(jnp.bfloat16)
-
-    pl.semaphore_wait(barrier, LEVELS)
-    for s in (1, 2, 3, 4, 0):
-        @pl.when(bit(s) == 0)
-        def _():
-            copy(s, -1).start()
+    def coarsen(part):
+        @pl.loop(part * (width // chunk // PARTS), (part + 1) * (width // chunk // PARTS))
+        def _(c):
+            columns = pl.ds(pl.multiple_of(c * chunk, chunk), chunk)
+            keys, values = k_ref[:, columns], v_ref[:, columns]
+            for s in range(LEVELS):
+                rows = BLOCK // 2**s
+                mean = halving(2 * rows)
+                keys = jnp.dot(mean, keys, preferred_element_type=jnp.float32)
+                values = jnp.dot(mean, values, preferred_element_type=jnp.float32)
+                pyramid[s][:, columns] = jnp.concatenate([keys, values], axis=0).astype(jnp.bfloat16)
+                keys, values = keys.astype(jnp.bfloat16), values.astype(jnp.bfloat16)
 
     def columns_of(h):
         return pl.ds(pl.multiple_of(h * HD, HD), HD)
 
-    def store(h, state):
-        tops[h] = state[0]
-        numerators[h] = state[1]
-        denominators[h] = state[2]
-
-    def local(h):
-        columns = columns_of(h)
+    def store(group, states):
+        for h, state in zip(group, states):
+            tops[h] = state[0]
+            numerators[h] = state[1]
+            denominators[h] = state[2]
+
+    def attend(items):
+        scores = [scores_of(keys, query) for keys, query, _, _ in items]
+        scores = [
+            s if item[3] is None else jnp.where(item[3], s, -jnp.inf) for s, item in zip(scores, items)
+        ]
+        soft = [softened(s) for s in scores]
+        sums = [weighted(item[2], weights) for item, (_, weights, _) in zip(items, soft)]
+        return [(top, n, total) for (top, _, total), n in zip(soft, sums)]
+
+    def local(group):
         key = lax.broadcasted_iota(jnp.int32, (BLOCK, BLOCK), 0)
         token = lax.broadcasted_iota(jnp.int32, (BLOCK, BLOCK), 1)
         causal = key <= token
-        low, high = pl.ds(0, BLOCK), pl.ds(BLOCK, BLOCK)
-
-        def level(block, rows, mask):
-            scores = scores_of(k_ref[rows, columns], q_ref[block, columns])
-            if mask:
-                scores = jnp.where(causal, scores, -jnp.inf)
-            top, weights, total = softened(scores)
-            return top, weighted(v_ref[rows, columns], weights), total
-
-        first = level(low, low, True)
-        second = merged(level(high, high, True), level(high, low, False))
-        store(h, [jnp.concatenate(two, axis=1) for two in zip(first, second)])
-
-    def far(s):
+        items = []
+        for h in group:
+            columns = columns_of(h)
+            query = [q_ref[pl.ds(r * BLOCK, BLOCK), columns] for r in range(2)]
+            keys = [k_ref[pl.ds(r * BLOCK, BLOCK), columns] for r in range(2)]
+            values = [v_ref[pl.ds(r * BLOCK, BLOCK), columns] for r in range(2)]
+            items += [
+                (keys[0], query[0], values[0], causal),
+                (keys[1], query[1], values[1], causal),
+                (keys[0], query[1], values[0], None),
+            ]
+        levels = attend(items)
+        states = []
+        for u in range(len(group)):
+            first, second = levels[3 * u], merged(levels[3 * u + 1], levels[3 * u + 2])
+            states.append([jnp.concatenate(two, axis=1) for two in zip(first, second)])
+        store(group, states)
+
+    def far(s, c):
         rows = BLOCK // 2**s
 
-        def of_head(h):
-            columns = columns_of(h)
-            if rows >= 16:
-                keys = tiles[s][:, :rows, columns].reshape(BLOCK, HD)
-                values = tiles[s][:, rows:, columns].reshape(BLOCK, HD)
-            else:
-                both = tiles[s][:, :, columns].astype(jnp.float32)
-                keys = both[:, :rows].reshape(BLOCK, HD).astype(jnp.bfloat16)
-                values = both[:, rows:].reshape(BLOCK, HD).astype(jnp.bfloat16)
-            top, weights, total = softened(scores_of(keys, q_ref[:, columns]))
-            level = (top + (s + 1.0), weighted(values, weights), total)
-            store(h, merged((tops[h], numerators[h], denominators[h]), level))
+        def of_group(group):
+            items = []
+            for h in group:
+                columns = columns_of(h)
+                if rows >= 16:
+                    keys = tiles[s][:, :rows, columns].reshape(BLOCK, HD)
+                    values = tiles[s][:, rows:, columns].reshape(BLOCK, HD)
+                else:
+                    both = tiles[s][:, :, columns].astype(jnp.float32)
+                    keys = both[:, :rows].reshape(BLOCK, HD).astype(jnp.bfloat16)
+                    values = both[:, rows:].reshape(BLOCK, HD).astype(jnp.bfloat16)
+                items.append((keys, q_ref[:, columns], values, None))
+            olds = [(tops[h], numerators[h], denominators[h]) for h in group]
+            levels = [(top + (s + 1.0), n, total) for top, n, total in attend(items)]
+            store(group, [merged(old, level) for old, level in zip(olds, levels)])
 
         @pl.when(bit(s) == 1)
         def _():
-            each(of_head)
-
-    def each(of_head):
-        @pl.loop(0, heads // UNROLL)
+            each(of_group, c)
+
+    def each(of_group, c):
+        count = heads // PARTS // UNROLL
+
+        @pl.loop(c * count, (c + 1) * count)
         def _(g):
-            for u in range(UNROLL):
-                of_head(g * UNROLL + u)
-
-    def final(h):
-        result = numerators[h] / denominators[h]
-        o_ref[:, columns_of(h)] = result.T.astype(o_ref.dtype)
-
-    each(local)
-    landed(3, -1)
-    landed(4, -1)
-    landed(0, -1)
-    far(0)
-    landed(2, -1)
-    landed(4, 0)
-    landed(3, 0)
-    landed(4, 1)
-    landed(1, -1)
-    landed(3, 1)
-    landed(1, 0)
-    far(1)
-    landed(2, 0)
-    landed(4, 2)
-    landed(3, 2)
-    far(3)
-    landed(2, 1)
-    far(2)
-    landed(4, 3)
-    far(4)
-    each(final)
-    for s, i in COPIES:
+            of_group([g * UNROLL + u for u in range(UNROLL)])
+
+    def final(group):
+        results = [(numerators[h] * (1.0 / denominators[h])).T.astype(o_ref.dtype) for h in group]
+        for h, result in zip(group, results):
+            o_ref[:, columns_of(h)] = result
+
+    coarsen(0)
+    pl.semaphore_wait(barrier, LEVELS)
+    for s in (4, 3, 2, 1, 0):
+        push(s, 0)
+    coarsen(1)
+    for s in (4, 3, 2, 0):
+        push(s, 1)
+    each(local, 0)
+    for c in range(PARTS):
+        landed(3, -1, c)
+        landed(4, -1, c)
+    each(local, 1)
+    landed(2, -1, 0)
+    landed(2, -1, 1)
+    push(1, 1)
+    landed(0, -1, 0)
+    far(0, 0)
+    landed(3, 0, 0)
+    landed(4, 0, 0)
+    landed(0, -1, 1)
+    far(0, 1)
+    landed(3, 0, 1)
+    landed(4, 0, 1)
+    landed(1, -1, 0)
+    landed(4, 1, 0)
+    landed(4, 1, 1)
+    landed(1, 0, 0)
+    far(1, 0)
+    landed(3, 1, 0)
+    landed(2, 0, 0)
+    landed(3, 1, 1)
+    landed(4, 2, 0)
+    landed(3, 2, 0)
+    far(3, 0)
+    landed(2, 1, 0)
+    far(2, 0)
+    landed(4, 2, 1)
+    landed(2, 0, 1)
+    landed(3, 2, 1)
+    far(3, 1)
+    landed(4, 3, 0)
+    far(4, 0)
+    each(final, 0)
+    landed(4, 3, 1)
+    far(4, 1)
+    landed(1, -1, 1)
+    landed(2, 1, 1)
+    far(2, 1)
+    landed(1, 0, 1)
+    far(1, 1)
+    each(final, 1)
+    for s, i, c in COPIES:
         @pl.when(bit(s) == (0 if i < 0 else 1))
         def _():
-            copy(s, i).wait_send()
-
-
-UNROLL = 2
+            copy(s, i, c).wait_send()
+
+
+UNROLL = 8
 
 
 def fused(head_bits, queries, keys, values):

time: 102 us -> 57.1 us (0.56)
  Pallas kernels: 98.7 us -> 53.7 us
    pallas_call x1, Pallas kernels: 98.7 us -> 53.7 us  [fused(): pl.pallas_call(functools.partial(kernel, head_bits), out_shape=jax.ShapeD...]
where the time goes in v1:
time: 57.1 us; the launch traced here: 56.7 us
  Pallas kernels  53.7 us (94%)
  local copies, waits for them, and re-layouts  2.91 us (5%)
    pallas_call x1, Pallas kernels, fused(): pl.pallas_call(functools.partial(kernel, head_bits), out_shape=jax.ShapeD...  53.7 us
    unnamed x3, local copies, waits for them, and re-layouts  2.91 us

profile of v1, /device:TPU:30, one launch (start us, length us, event | category | flops | bytes accessed | tf_op | source)
XLA Modules:
  0.0 56.7 jit_solution(1964702520993155615)
XLA Ops:
  0.0 0.0 copy-start
  0.0 1.6 %copy-done = bf16[256,4096]{1,0:T(8,128)(2,1)S(1)} copy-done((bf16[256,4096]{1,0:T(8,128)(2,1)S(1)}, bf16[256,4096]{1,0:T(8,128)(2,1)}, u32[]{:S(2)}) %copy-start) | copy-done | bytes 2097176
  1.6 53.7 %shard_map.37 = bf16[256,4096]{1,0:T(8,128)(2,1)S(1)} custom-call(bf16[256,4096]{1,0:T(8,128)(2,1)S(1)} %copy-done, bf16[256,4096]{1,0:T(8,128)(2,1)} %k_ref.1, bf16[256,4096]{1,0:T(8,128)(2,1)} %v_ref.1), custom_call_target="tpu_custom_call" | custom-call | tf_op jit(solution)/shard_map/pallas_call | solution.py:431
  55.3 1.3 %copy.5 = bf16[256,4096]{1,0:T(8,128)(2,1)} copy(bf16[256,4096]{1,0:T(8,128)(2,1)S(1)} %shard_map.37) | data formatting | bytes 4194304
Async XLA Ops:
  0.0 1.6 %copy-start = (bf16[256,4096]{1,0:T(8,128)(2,1)S(1)}, bf16[256,4096]{1,0:T(8,128)(2,1)}, u32[]{:S(2)}) copy-start(bf16[256,4096]{1,0:T(8,128)(2,1)} %q_ref.1) | copy-start | bytes 6291460

commit v2 on v1

--- a/solution.py
+++ b/solution.py
@@ -397,10 +397,10 @@
     far(3, 1)
     landed(4, 3, 0)
     far(4, 0)
+    landed(1, -1, 1)
     each(final, 0)
     landed(4, 3, 1)
     far(4, 1)
-    landed(1, -1, 1)
     landed(2, 1, 1)
     far(2, 1)
     landed(1, 0, 1)

time: 57.1 us -> 57.8 us (1.012)
  Pallas kernels: 53.7 us -> 54.8 us
    pallas_call x1, Pallas kernels: 53.7 us -> 54.8 us  [fused(): pl.pallas_call(functools.partial(kernel, head_bits), out_shape=jax.ShapeD...]
where the time goes in v2:
time: 57.8 us; the launch traced here: 57.7 us
  Pallas kernels  54.8 us (95%)
  local copies, waits for them, and re-layouts  2.91 us (5%)
    pallas_call x1, Pallas kernels, fused(): pl.pallas_call(functools.partial(kernel, head_bits), out_shape=jax.ShapeD...  54.8 us
    unnamed x3, local copies, waits for them, and re-layouts  2.91 us

profile of v2, /device:TPU:30, one launch (start us, length us, event | category | flops | bytes accessed | tf_op | source)
XLA Modules:
  0.0 57.7 jit_solution(4075615265070596495)
XLA Ops:
  0.0 0.0 copy-start
  0.0 1.6 %copy-done = bf16[256,4096]{1,0:T(8,128)(2,1)S(1)} copy-done((bf16[256,4096]{1,0:T(8,128)(2,1)S(1)}, bf16[256,4096]{1,0:T(8,128)(2,1)}, u32[]{:S(2)}) %copy-start) | copy-done | bytes 2097176
  1.6 54.8 %shard_map.37 = bf16[256,4096]{1,0:T(8,128)(2,1)S(1)} custom-call(bf16[256,4096]{1,0:T(8,128)(2,1)S(1)} %copy-done, bf16[256,4096]{1,0:T(8,128)(2,1)} %k_ref.1, bf16[256,4096]{1,0:T(8,128)(2,1)} %v_ref.1), custom_call_target="tpu_custom_call" | custom-call | tf_op jit(solution)/shard_map/pallas_call | solution.py:431
  56.4 1.3 %copy.5 = bf16[256,4096]{1,0:T(8,128)(2,1)} copy(bf16[256,4096]{1,0:T(8,128)(2,1)S(1)} %shard_map.37) | data formatting | bytes 4194304
Async XLA Ops:
  0.0 1.6 %copy-start = (bf16[256,4096]{1,0:T(8,128)(2,1)S(1)}, bf16[256,4096]{1,0:T(8,128)(2,1)}, u32[]{:S(2)}) copy-start(bf16[256,4096]{1,0:T(8,128)(2,1)} %q_ref.1) | copy-start | bytes 6291460

commit v3 on v1

--- a/solution.py
+++ b/solution.py
@@ -249,11 +249,37 @@
             device_id=partner(b), device_id_type=MESH,
         )
 
+    def relayed():
+        part = pl.ds(0, width // PARTS)
+        return pltpu.make_async_remote_copy(
+            src_ref=tiles[2].at[slot(2) - 1, :, part], dst_ref=tiles[2].at[slot(2) - 1, :, part],
+            send_sem=send_sems.at[COPIES.index((2, 0, 0))], recv_sem=recv_sems.at[COPIES.index((2, 0, 0))],
+            device_id=partner(2), device_id_type=MESH,
+        )
+
+    def relay():
+        @pl.when((1 - bit(2)) * bit(1) == 1)
+        def _():
+            @pl.loop(0, width // chunk // PARTS)
+            def _(c):
+                columns = pl.ds(pl.multiple_of(c * chunk, chunk), chunk)
+                mean = halving(64)
+                held = tiles[1].at[slot(1)]
+                keys = jnp.dot(mean, held[:64, columns], preferred_element_type=jnp.float32)
+                values = jnp.dot(mean, held[64:, columns], preferred_element_type=jnp.float32)
+                tiles[2][slot(2) - 1, :, columns] = jnp.concatenate([keys, values], axis=0).astype(jnp.bfloat16)
+
+            relayed().start()
+
     def landed(s, i, c):
         @pl.when(bit(s) == 1)
         def _():
             copy(s, i, c).wait_recv()
-            if i + 1 < s:
+            if (s, i, c) == (2, -1, 0):
+                @pl.when(bit(1) == 1)
+                def _():
+                    copy(2, 0, 0).start()
+            elif i + 1 < s:
                 copy(s, i + 1, c).start()
 
     def push(s, c):
@@ -379,6 +405,7 @@
     landed(3, 0, 1)
     landed(4, 0, 1)
     landed(1, -1, 0)
+    relay()
     landed(4, 1, 0)
     landed(4, 1, 1)
     landed(1, 0, 0)
@@ -407,9 +434,15 @@
     far(1, 1)
     each(final, 1)
     for s, i, c in COPIES:
-        @pl.when(bit(s) == (0 if i < 0 else 1))
+        sends = bit(s) * bit(1) if (s, i, c) == (2, 0, 0) else bit(s) if i >= 0 else 1 - bit(s)
+
+        @pl.when(sends == 1)
         def _():
             copy(s, i, c).wait_send()
+
+    @pl.when((1 - bit(2)) * bit(1) == 1)
+    def _():
+        relayed().wait_send()
 
 
 UNROLL = 8

time: 57.1 us -> 59.6 us (1.044)
  Pallas kernels: 53.7 us -> 56.2 us
    pallas_call x1, Pallas kernels: 53.7 us -> 56.2 us  [fused(): pl.pallas_call(functools.partial(kernel, head_bits), out_shape=jax.ShapeD...]
where the time goes in v3:
time: 59.6 us; the launch traced here: 59.1 us
  Pallas kernels  56.2 us (94%)
  local copies, waits for them, and re-layouts  2.91 us (5%)
    pallas_call x1, Pallas kernels, fused(): pl.pallas_call(functools.partial(kernel, head_bits), out_shape=jax.ShapeD...  56.2 us
    unnamed x3, local copies, waits for them, and re-layouts  2.91 us

profile of v3, /device:TPU:30, one launch (start us, length us, event | category | flops | bytes accessed | tf_op | source)
XLA Modules:
  0.0 59.1 jit_solution(1333399012597107027)
XLA Ops:
  0.0 0.0 copy-start
  0.0 1.6 %copy-done = bf16[256,4096]{1,0:T(8,128)(2,1)S(1)} copy-done((bf16[256,4096]{1,0:T(8,128)(2,1)S(1)}, bf16[256,4096]{1,0:T(8,128)(2,1)}, u32[]{:S(2)}) %copy-start) | copy-done | bytes 2097176
  1.6 56.2 %shard_map.37 = bf16[256,4096]{1,0:T(8,128)(2,1)S(1)} custom-call(bf16[256,4096]{1,0:T(8,128)(2,1)S(1)} %copy-done, bf16[256,4096]{1,0:T(8,128)(2,1)} %k_ref.1, bf16[256,4096]{1,0:T(8,128)(2,1)} %v_ref.1), custom_call_target="tpu_custom_call" | custom-call | tf_op jit(solution)/shard_map/pallas_call | solution.py:464
  57.8 1.3 %copy.5 = bf16[256,4096]{1,0:T(8,128)(2,1)} copy(bf16[256,4096]{1,0:T(8,128)(2,1)S(1)} %shard_map.37) | data formatting | bytes 4194304
Async XLA Ops:
  0.0 1.6 %copy-start = (bf16[256,4096]{1,0:T(8,128)(2,1)S(1)}, bf16[256,4096]{1,0:T(8,128)(2,1)}, u32[]{:S(2)}) copy-start(bf16[256,4096]{1,0:T(8,128)(2,1)} %q_ref.1) | copy-start | bytes 6291460
